TPU v7x, 32 devices: a whole 2x2x4 slice. The times are simulated.
32 devices in a mesh: groups: 2 (over y), seq: 16 (over z, x, core).
Axes of the slice: x: 2, y: 2, z: 4, core: 2. Of those that a mesh axis runs over, the one named last changes fastest.
Arguments:
- acts: bfloat16 [256, 2048], P(('groups', 'seq')), parts along dimension 0, may hold values from -6 to 6
- grads: bfloat16 [256, 2048], P(('groups', 'seq')), parts along dimension 0, may hold values from -6 to 6
- basis_in: bfloat16 [2048, 2048], P('seq'), may hold values from -0.125 to 0.125
- basis_out: bfloat16 [2048, 2048], P('seq'), may hold values from -0.125 to 0.125
- eigvals: float32 [2048, 2048], P('seq'), may hold values from 0.02 to 0.5
Outputs:
- preconditioned: bfloat16 [2048, 2, 2048], P('seq', 'groups'), parts along dimension 1
There are 2 independent parts, one for each index of `groups`. A program takes and returns all parts, laid end to end along the dimension named above; an argument that names none is the same for every part. Nothing has to cross between parts.
All inputs are finite; a program needn't handle non-finite values.
Results may differ from a plain program's by a relative error of at most 0.0059.
Values may be sent and summed in bfloat16 or wider, within the bound.
A program may use at most 128 MiB of HBM per device.

v0:
```python
import jax
import jax.numpy as jnp
from jax import lax
from jax.sharding import PartitionSpec as P

QLEN = 128


DAMPING = 0.01


def body(acts, grads, basis_in, basis_out, eigvals):
    parts = lax.axis_size("seq")
    cols = eigvals.shape[0]
    width = eigvals.shape[1]
    full_in, full_out = (
        lax.all_gather(basis_in, "seq", axis=0, tiled=True),
        lax.all_gather(basis_out, "seq", axis=0, tiled=True),
    )
    rot_in = jnp.dot(acts, full_in, preferred_element_type=jnp.float32).astype(jnp.bfloat16)
    rot_out = jnp.dot(grads, full_out, preferred_element_type=jnp.float32).astype(jnp.bfloat16)
    queries = rot_in.shape[0] * parts // QLEN
    in_cols = lax.all_to_all(rot_in, "seq", split_axis=1, concat_axis=0, tiled=True)
    out_all = lax.all_gather(rot_out, "seq", axis=0, tiled=True)
    raw = jnp.einsum(
        "qlc,qld->cqd",
        in_cols.reshape(queries, QLEN, cols),
        out_all.reshape(queries, QLEN, width),
        preferred_element_type=jnp.float32,
    )
    scaled = (raw / (QLEN * (eigvals[:, None, :] + DAMPING))).astype(jnp.bfloat16)
    by_cols = lax.all_to_all(scaled, "seq", split_axis=2, concat_axis=0, tiled=True)
    left = jnp.dot(
        full_in, by_cols.reshape(width, queries * cols), preferred_element_type=jnp.float32
    )
    left = left.astype(jnp.bfloat16).reshape(width, queries, cols)
    left_rows = lax.all_to_all(left, "seq", split_axis=0, concat_axis=2, tiled=True)
    result = lax.dot_general(
        left_rows.reshape(cols * queries, width),
        full_out,
        (((1,), (1,)), ((), ())),
        preferred_element_type=jnp.float32,
    )
    return result.reshape(cols, queries, width).astype(jnp.bfloat16)


def solution(mesh):
    return jax.shard_map(
        body,
        mesh=mesh,
        in_specs=(
            P(("groups", "seq"), None),
            P(("groups", "seq"), None),
            P("seq", None),
            P("seq", None),
            P("seq", None),
        ),
        out_specs=P("seq", "groups", None),
        check_vma=False,
    )
```

profile of v0, /device:TPU:0, one launch (start us, length us, event | category | flops | bytes accessed | tf_op | source)
XLA Modules:
  0.0 267.5 jit_solution(6174395085380230618)
XLA Ops:
  6.5 0.7 all-gather.5.cloned.1.call-update
  7.3 0.7 all-gather.3.cloned.1.call-update
  8.0 1.5 copy.13
  9.6 77.6 %all-gather.5.cloned.1.call-done = bf16[2048,2048]{1,0:T(8,128)(2,1)} async-done(((bf16[128,2048]{1,0:T(8,128)(2,1)}), bf16[2048,2048]{1,0:T(8,128)(2,1)}) %all-gather.5.cloned.1.call-update) | async-done | bytes 8388624 | tf_op jit(solution)/shard_map/all_gather | solution.py:17
  87.1 5.2 %fusion.4 = bf16[8,16,128]{2,0,1:T(8,128)(2,1)} fusion(bf16[8,2048]{1,0:T(8,128)(2,1)S(1)} %copy-done, bf16[2048,2048]{1,0:T(8,128)(2,1)} %all-gather.5.cloned.1.call-done), kind=kOutput, calls=%fused_computation.9 | convolution fusion | flops 67125248 | bytes 8454144 | tf_op jit(solution)/shard_map/dot_general | solution.py:20
  92.3 3.5 %all-to-all-start = ((bf16[8,16,128]{2,0,1:T(8,128)(2,1)}), bf16[8,16,128]{2,0,1:T(8,128)(2,1)S(1)}, u32[]{:S(2)}, u32[]{:S(2)}) async-start(bf16[8,16,128]{2,0,1:T(8,128)(2,1)} %fusion.4), calls=%async_computation | async-start | bytes 65536 | tf_op jit(solution)/shard_map/all_to_all | solution.py:23
  95.8 67.3 %all-gather.3.cloned.1.call-done = bf16[2048,2048]{1,0:T(8,128)(2,1)} async-done(((bf16[128,2048]{1,0:T(8,128)(2,1)}), bf16[2048,2048]{1,0:T(8,128)(2,1)}) %all-gather.3.cloned.1.call-update) | async-done | bytes 8388624 | tf_op jit(solution)/shard_map/all_gather | solution.py:18
  163.1 4.6 %convolution_convert_fusion.3 = bf16[8,2048]{1,0:T(8,128)(2,1)S(1)} fusion(bf16[8,2048]{1,0:T(8,128)(2,1)S(1)} %copy-done.1, bf16[2048,2048]{1,0:T(8,128)(2,1)} %all-gather.3.cloned.1.call-done), kind=kOutput, calls=%fused_computation.6 | convolution fusion | flops 67125248 | bytes 8454144 | tf_op jit(solution)/shard_map/dot_general | solution.py:21
  167.7 20.3 %all_gather.10 = bf16[128,2048]{1,0:T(8,128)(2,1)S(1)} all-gather(bf16[8,2048]{1,0:T(8,128)(2,1)S(1)} %convolution_convert_fusion.3), channel_id=1, replica_groups=mesh['groups'=2,'seq'=16] {'seq'}, dimensions={0}, use_global_device_ids=true | all-gather | bytes 557056 | tf_op jit(solution)/shard_map/all_gather | solution.py:24
  188.0 0.3 fusion.3
  188.4 8.1 %copy.21 = bf16[128,1,2048]{0,1,2:T(2,128)(2,1)S(1)} copy(bf16[128,1,2048]{0,2,1:T(8,128)(2,1)S(1)} %fusion.3) | data formatting | bytes 1048576 | tf_op jit(solution)/shard_map/convert_element_type | solution.py:31
  196.5 0.5 broadcast.2
  197.0 11.5 %reduce = bf16[2048,128]{1,0:T(8,128)(2,1)S(1)} reduce(bf16[2048,1,128]{2,1,0:T(2,128)(2,1)S(1)} %bitcast.45, bf16[]{:T(256)} %broadcast.2), dimensions={1}, to_apply=%bitcast.43.reduce_sub_computation | reduce | bytes 1048578
  208.7 17.1 %all_to_all.46 = bf16[16,2,8192]{2,1,0:T(2,128)(2,1)S(1)} all-to-all(bf16[16,2,8192]{2,1,0:T(2,128)(2,1)S(1)} %reshape.32), channel_id=1, replica_groups=mesh['groups'=2,'seq'=16] {'seq'}, dimensions={0} | all-to-all | bytes 1048576 | tf_op jit(solution)/shard_map/all_to_all | solution.py:32
  225.8 0.5 reshape.33
  226.4 0.3 copy.15
  226.7 6.3 %fusion = bf16[2048,1,128]{0,2,1:T(8,128)(2,1)S(1)} fusion(bf16[2048,128]{1,0:T(8,128)(2,1)S(1)} %bitcast.46, bf16[2048,2048]{1,0:T(8,128)(2,1)} %all-gather.5.cloned.1.call-done), kind=kOutput, calls=%fused_computation.3 | convolution fusion | flops 1074003968 | bytes 9437184 | tf_op jit(solution)/shard_map/dot_general | solution.py:33
  233.0 1.0 reduce.1
  234.0 0.3 copy.22
  234.2 0.1 reshape.34
  234.4 18.3 %all_to_all.47 = bf16[16,2,8192]{2,1,0:T(2,128)(2,1)S(1)} all-to-all(bf16[16,2,8192]{2,1,0:T(2,128)(2,1)S(1)} %reshape.34), channel_id=1, replica_groups=mesh['groups'=2,'seq'=16] {'seq'}, dimensions={0} | all-to-all | bytes 1048576 | tf_op jit(solution)/shard_map/all_to_all | solution.py:37
  252.7 0.5 reshape.35
  253.3 0.3 copy.17
  253.5 7.1 %fusion.1 = bf16[128,1,2048]{2,0,1:T(8,128)(2,1)} fusion(bf16[128,2048]{0,1:T(8,128)(2,1)S(1)} %bitcast.47, bf16[2048,2048]{1,0:T(8,128)(2,1)} %all-gather.3.cloned.1.call-done), kind=kOutput, calls=%fused_computation.4 | convolution fusion | flops 1074003968 | bytes 9437184 | tf_op jit(solution)/shard_map/dot_general | solution.py:38
  (10 shorter events, 0.3 us)
Async XLA Ops:
  6.5 80.6 %copy-start = (bf16[8,2048]{1,0:T(8,128)(2,1)S(1)}, bf16[8,2048]{1,0:T(8,128)(2,1)}, u32[]{:S(2)}) copy-start(bf16[8,2048]{1,0:T(8,128)(2,1)} %param.5) | copy-start | bytes 98308
  6.5 80.6 %all-gather.5.cloned.1.call-start = ((), (), s32[]{:S(2)}) async-start(), calls=%async_computation.4 | async-start | bytes 8912896 | tf_op jit(solution)/shard_map/all_gather | solution.py:17
  7.3 155.9 %all-gather.3.cloned.1.call-start = ((), (), s32[]{:S(2)}) async-start(), calls=%async_computation.3 | async-start | bytes 8912896 | tf_op jit(solution)/shard_map/all_gather | solution.py:18
  9.6 153.6 %copy-start.1 = (bf16[8,2048]{1,0:T(8,128)(2,1)S(1)}, bf16[8,2048]{1,0:T(8,128)(2,1)}, u32[]{:S(2)}) copy-start(bf16[8,2048]{1,0:T(8,128)(2,1)} %param.6) | copy-start | bytes 98308
  92.3 95.7 %all-to-all-start = ((bf16[8,16,128]{2,0,1:T(8,128)(2,1)}), bf16[8,16,128]{2,0,1:T(8,128)(2,1)S(1)}, u32[]{:S(2)}, u32[]{:S(2)}) async-start(bf16[8,16,128]{2,0,1:T(8,128)(2,1)} %fusion.4), calls=%async_computation | async-start | bytes 65536 | tf_op jit(solution)/shard_map/all_to_all | solution.py:23
Sparse Core Ops, SparseCore 0:
  9.5 77.5 all-gather.4
  89.3 73.7 all-gather.2
where the time goes:
time: 268 us; the launch traced here: 267 us
  waiting for transfers between devices  146 us (54%)
  blocking collectives  55.7 us (21%)
  matrix products  23.5 us (9%)
  between operations  13.5 us (5%)
  local copies, waits for them, and re-layouts  12.5 us (5%)
  other arithmetic  12.5 us (5%)
  starting transfers between devices  3.54 us (1%)
    all_gather x1, waiting for transfers between devices, body(): lax.all_gather(basis_in, 'seq', axis=0, tiled=True)  77.6 us
    all_gather x1, waiting for transfers between devices, body(): lax.all_gather(basis_out, 'seq', axis=0, tiled=True)  67.3 us
    all_gather x1, blocking collectives, body(): out_all = lax.all_gather(rot_out, 'seq', axis=0, tiled=True)  20.3 us
    all_to_all x1, blocking collectives, body(): lax.all_to_all(left, 'seq', split_axis=0, concat_axis=2, tiled=True)  18.3 us
    all_to_all x1, blocking collectives, body(): lax.all_to_all(scaled, 'seq', split_axis=2, concat_axis=0, tiled=True)  17.1 us
    unnamed x1, other arithmetic  11.5 us
    convert_element_type x1, local copies, waits for them, and re-layouts, body(): (raw / (QLEN * (eigvals[:, None, :] + DAMPING))).astype(jnp.bfloat16)  8.14 us
    dot_general x1, matrix products, body(): lax.dot_general(left_rows.reshape(cols * queries, width), full_out, (((1,...  7.1 us
  transfers between devices with their start and end apart: 3, of which 2 were waited for; matrix products, arithmetic and copies ran while one was open for 4% of the time, Pallas kernels for 0%

commit v1 on v0

--- a/solution.py
+++ b/solution.py
@@ -1,12 +1,264 @@
+import functools
+
 import jax
 import jax.numpy as jnp
 from jax import lax
+from jax.experimental import pallas as pl
+from jax.experimental.pallas import tpu as pltpu
 from jax.sharding import PartitionSpec as P
 
 QLEN = 128
-
-
 DAMPING = 0.01
+MESH = pl.DeviceIdType.MESH
+F32, BF16 = jnp.float32, jnp.bfloat16
+
+
+def flip(v, d):
+    return 1 - v if d else v
+
+
+def kernel(ag, bin_, bout, eig, out,
+           ag_all, ebf, epan, bpan, binpan, part, rq, zpart, rz, rotq, rin, rout,
+           sbuf, left, leftx, psend, precv, ptmp,
+           ag_s, ag_r, sl_s, sl_r, q_s, q_r, z_s, z_r, g_s, g_r,
+           up_s, dn_s, blk_r, bi_s, bi_r, qy_s, qy_r, ro_s, ro_r, bo_s, bo_r, le_s, le_r, p_s, p_r):
+    y = lax.axis_index("groups")
+    s = lax.axis_index("seq")
+    z, x, c = s // 4, (s // 2) % 2, s % 2
+    q = s % 4
+
+    def dev(zz, xx, cc, yy):
+        return (yy, zz * 4 + xx * 2 + cc)
+
+    def rc(src, dst, ss, rs, to):
+        return pltpu.make_async_remote_copy(
+            src_ref=src, dst_ref=dst, send_sem=ss, recv_sem=rs, device_id=to, device_id_type=MESH)
+
+    def arrived(dst, rs):
+        rc(dst, dst, rs, rs, dev(z, x, 1 - c, y)).wait_recv()
+
+    def sent(src, ss):
+        rc(src, src, ss, ss, dev(z, x, 1 - c, y)).wait_send()
+
+    QP = ((0, 1), (1, 0), (1, 1))
+
+    barrier = pltpu.get_barrier_semaphore()
+    for d in range(1, 16):
+        pl.semaphore_signal(barrier, inc=1, device_id=(y, (s + d) % 16), device_id_type=MESH)
+    for i in range(4):
+        pl.semaphore_signal(barrier, inc=1, device_id=(1 - y, z * 4 + i), device_id_type=MESH)
+    pl.semaphore_wait(barrier, 19)
+
+    pend = []
+    for d in range(1, 16):
+        t = (s + d) % 16
+        cp = rc(ag.at[:, pl.ds(pl.multiple_of(t * 128, 128), 128)], ag_all.at[s], ag_s.at[d], ag_r.at[16 - d],
+                (y, t))
+        cp.start()
+        pend.append(cp)
+    ag_all[s] = ag[:, pl.ds(pl.multiple_of(s * 128, 128), 128)]
+    ebf[...] = (1.0 / (QLEN * (eig[...] + DAMPING))).astype(BF16)
+
+    rows = pl.ds(pl.multiple_of(q * 128, 128), 128)
+    for i, (dx, dc) in enumerate(QP):
+        xx, cc = flip(x, dx), flip(c, dc)
+        cols = pl.ds(pl.multiple_of((xx * 4 + cc * 2 + y) * 256, 256), 256)
+        for k, (src, dst) in enumerate(((ebf, epan), (bout, bpan.at[0]))):
+            cp = rc(src.at[:, cols], dst.at[z, rows], sl_s.at[i, k], sl_r.at[i, k], dev(z, xx, cc, y))
+            cp.start()
+            pend.append(cp)
+    own = pl.ds(pl.multiple_of((q * 2 + y) * 256, 256), 256)
+    epan[z, rows] = ebf[:, own]
+    bpan[0, z, rows] = bout[:, own]
+
+    for d in range(1, 16):
+        arrived(ag_all.at[(s + d) % 16], ag_r.at[d])
+    tok = ag_all[...].reshape(256, 128)
+    for n in range(4):
+        cs = slice(n * 512, n * 512 + 512)
+        a = jnp.dot(tok, bin_[:, cs], preferred_element_type=F32).reshape(16, 16, 512)
+        part[n, :128] = a[:, :8].reshape(128, 512).astype(BF16)
+        b = jnp.dot(tok, bout[:, cs], preferred_element_type=F32).reshape(16, 16, 512)
+        part[n, 128:] = b[:, 8:].reshape(128, 512).astype(BF16)
+    for i, (dx, dc) in enumerate(QP):
+        xx, cc = flip(x, dx), flip(c, dc)
+        cp = rc(part.at[xx * 2 + cc], rq.at[i], q_s.at[i], q_r.at[i], dev(z, xx, cc, y))
+        cp.start()
+        pend.append(cp)
+
+    for i, (dx, dc) in enumerate(QP):
+        src = pl.ds(pl.multiple_of((flip(x, dx) * 2 + flip(c, dc)) * 128, 128), 128)
+        arrived(epan.at[z, src], sl_r.at[i, 0])
+        arrived(bpan.at[0, z, src], sl_r.at[i, 1])
+
+    def hop(j):
+        for up, sems in ((True, up_s), (False, dn_s)):
+            b = z - j if up else z + j
+            ok = (b >= 0) if up else (b <= 3)
+            nxt = z + 1 if up else z - 1
+            can = (z < 3) if up else (z > 0)
+            for k, ref in enumerate((epan, bpan.at[0])):
+                if j > 0:
+                    @pl.when(ok)
+                    def _():
+                        arrived(ref.at[b], blk_r.at[b, k])
+                if j < 3:
+                    @pl.when(ok & can)
+                    def _():
+                        rc(ref.at[b], ref.at[b], sems.at[j, k], blk_r.at[b, k], dev(nxt, x, c, y)).start()
+
+    def hop_sent():
+        for j in range(3):
+            for up, sems in ((True, up_s), (False, dn_s)):
+                b = z - j if up else z + j
+                ok = (b >= 0) if up else (b <= 3)
+                can = (z < 3) if up else (z > 0)
+
+                @pl.when(ok & can)
+                def _():
+                    for k, ref in enumerate((epan, bpan.at[0])):
+                        sent(ref.at[b], sems.at[j, k])
+
+    hop(0)
+
+    tot = part[q].astype(F32)
+    for i in range(3):
+        arrived(rq.at[i], q_r.at[i])
+        tot = tot + rq[i].astype(F32)
+    for i in range(4):
+        zpart[i] = tot[:, i * 128:(i + 1) * 128].astype(BF16)
+    for d in range(1, 4):
+        zz = (z + d) % 4
+        cp = rc(zpart.at[zz], rz.at[4 - d], z_s.at[d], z_r.at[4 - d], dev(zz, x, c, y))
+        cp.start()
+        pend.append(cp)
+
+    slot = c * 2 + x
+    binpan[slot] = bin_[...]
+    for i, to in enumerate((dev(z, x, 1 - c, y), dev(z, 1 - x, c, y))):
+        cp = rc(bin_, binpan.at[slot], bi_s.at[i], bi_r.at[i], to)
+        cp.start()
+        pend.append(cp)
+
+    tot = zpart[z].astype(F32)
+    for d in range(1, 4):
+        arrived(rz.at[d], z_r.at[d])
+        tot = tot + rz[d].astype(F32)
+    rotq[z] = tot.astype(BF16)
+    for d in range(1, 4):
+        zz = (z + d) % 4
+        cp = rc(rotq.at[z], rotq.at[z], g_s.at[d], g_r.at[4 - d], dev(zz, x, c, y))
+        cp.start()
+        pend.append(cp)
+    hop(1)
+    for d in range(1, 4):
+        arrived(rotq.at[(z + d) % 4], g_r.at[d])
+
+    rin[y, q] = rotq[:, :128]
+    rout[y] = rotq[pl.ds(2 * y, 2), 128:]
+    for i in range(1, 8):
+        dy, dx, dc = i // 4, (i // 2) % 2, i % 2
+        cp = rc(rotq.at[:, pl.ds(0, 128)], rin.at[y, q], qy_s.at[i], qy_r.at[i],
+                dev(z, flip(x, dx), flip(c, dc), flip(y, dy)))
+        cp.start()
+        pend.append(cp)
+    cp = rc(rotq.at[pl.ds(2 * (1 - y), 2), pl.ds(128, 128)], rout.at[y], ro_s.at[0], ro_r.at[0],
+            dev(z, x, c, 1 - y))
+    cp.start()
+    pend.append(cp)
+
+    far = c * 2 + 1 - x
+    arrived(binpan.at[far], bi_r.at[1])
+    cp = rc(binpan.at[far], binpan.at[far], bi_s.at[2], bi_r.at[2], dev(z, x, 1 - c, y))
+    cp.start()
+    pend.append(cp)
+
+    hop(2)
+    hop(3)
+    for i, to in ((1, dev(z, x, 1 - c, y)), (2, dev(z, x, c, 1 - y))):
+        cp = rc(bpan.at[0], bpan.at[i], bo_s.at[i], bo_r.at[i], to)
+        cp.start()
+        pend.append(cp)
+
+    for i in range(1, 8):
+        dy, dx, dc = i // 4, (i // 2) % 2, i % 2
+        arrived(rin.at[flip(y, dy), flip(x, dx) * 2 + flip(c, dc)], qy_r.at[i])
+    arrived(rout.at[1 - y], ro_r.at[0])
+
+    for g in range(2):
+        ro = jnp.concatenate([rout[g, 0], rout[g, 1]], axis=1)
+        for m in range(4):
+            for t in range(4):
+                raw = lax.dot_general(rin[g, m, t], ro, (((0,), (0,)), ((), ())), preferred_element_type=F32)
+                e = epan[m, t * 128:(t + 1) * 128].astype(F32)
+                sbuf[m * 512 + t * 128:m * 512 + (t + 1) * 128, g * 256:(g + 1) * 256] = (raw * e).astype(BF16)
+
+    arrived(binpan.at[(1 - c) * 2 + x], bi_r.at[0])
+    arrived(binpan.at[(1 - c) * 2 + 1 - x], bi_r.at[2])
+    for i in range(4):
+        l = jnp.dot(binpan[i], sbuf[...], preferred_element_type=F32).astype(BF16)
+        left[0, i] = l[:, :256]
+        left[1, i] = l[:, 256:]
+    for i in range(1, 4):
+        dy, dc = i // 2, i % 2
+        yy, cc = flip(y, dy), flip(c, dc)
+        cp = rc(left.at[yy, pl.ds(cc * 2, 2)], leftx.at[i], le_s.at[i], le_r.at[i], dev(z, x, cc, yy))
+        cp.start()
+        pend.append(cp)
+    leftx[0] = left[y, pl.ds(c * 2, 2)]
+
+    arrived(bpan.at[2], bo_r.at[2])
+    cp = rc(bpan.at[2], bpan.at[3], bo_s.at[3], bo_r.at[3], dev(z, x, 1 - c, y))
+    cp.start()
+    pend.append(cp)
+    arrived(bpan.at[1], bo_r.at[1])
+    for i in range(1, 4):
+        arrived(leftx.at[i], le_r.at[i])
+    arrived(bpan.at[3], bo_r.at[3])
+
+    for n in range(4):
+        acc = jnp.zeros((256, 512), F32)
+        for i in range(4):
+            acc = acc + lax.dot_general(leftx[i].reshape(256, 256), bpan[i, n], (((1,), (1,)), ((), ())),
+                                        preferred_element_type=F32)
+        ptmp[n] = acc.reshape(2, 128, 512)
+        psend[n] = ptmp[n, 1 - x].astype(BF16)
+        cp = rc(psend.at[n], precv.at[n], p_s.at[n], p_r.at[n], dev(z, 1 - x, c, y))
+        cp.start()
+        pend.append(cp)
+    for n in range(4):
+        arrived(precv.at[n], p_r.at[n])
+        out[:, n * 512:(n + 1) * 512] = (ptmp[n, x] + precv[n].astype(F32)).astype(BF16)
+
+    for cp in pend:
+        cp.wait_send()
+    hop_sent()
+
+
+def fused(acts, grads, basis_in, basis_out, eigvals):
+    ag = jnp.concatenate([acts, grads], axis=0)
+    v = pltpu.VMEM
+    dma = lambda *n: pltpu.SemaphoreType.DMA(n)
+    out = pl.pallas_call(
+        kernel,
+        out_shape=jax.ShapeDtypeStruct((128, 2048), BF16),
+        in_specs=[pl.BlockSpec(memory_space=v)] * 4,
+        out_specs=pl.BlockSpec(memory_space=v),
+        scratch_shapes=[
+            v((16, 16, 128), BF16), v((128, 2048), BF16), v((4, 512, 256), BF16), v((4, 4, 512, 256), BF16),
+            v((4, 128, 2048), BF16), v((4, 256, 512), BF16), v((3, 256, 512), BF16), v((4, 256, 128), BF16),
+            v((4, 256, 128), BF16), v((4, 256, 128), BF16), v((2, 4, 4, 128, 128), BF16), v((2, 2, 128, 128), BF16),
+            v((2048, 512), BF16), v((2, 4, 128, 256), BF16), v((4, 2, 128, 256), BF16),
+            v((4, 128, 512), BF16), v((4, 128, 512), BF16), v((4, 2, 128, 512), F32),
+            dma(16), dma(16), dma(3, 2), dma(3, 2), dma(3), dma(3), dma(4), dma(4), dma(4), dma(4),
+            dma(3, 2), dma(3, 2), dma(4, 2), dma(3), dma(3), dma(8), dma(8), dma(1), dma(1), dma(4), dma(4),
+            dma(4), dma(4), dma(4), dma(4),
+        ],
+        compiler_params=pltpu.CompilerParams(
+            collective_id=0, has_side_effects=True, vmem_limit_bytes=48 * 1024 * 1024),
+        cost_estimate=pl.CostEstimate(flops=5 * 10**9, bytes_accessed=3 * 10**6, transcendentals=0),
+    )(ag, basis_in, basis_out, eigvals)
+    return out.reshape(128, 1, 2048)
 
 
 def body(acts, grads, basis_in, basis_out, eigvals):
@@ -45,8 +297,13 @@
 
 
 def solution(mesh):
+    small = mesh.shape["seq"] == 16 and mesh.shape["groups"] == 2
+
+    def step(acts, *rest):
+        return (fused if small and acts.shape == (8, 2048) else body)(acts, *rest)
+
     return jax.shard_map(
-        body,
+        step,
         mesh=mesh,
         in_specs=(
             P(("groups", "seq"), None),

time: 268 us -> 110 us (0.41)
  waiting for transfers between devices: 146 us -> 0 us
  Pallas kernels: 0 us -> 105 us
  blocking collectives: 55.7 us -> 0 us
  matrix products: 23.5 us -> 0 us
  between operations: 13.5 us -> 0.01 us
  other arithmetic: 12.5 us -> 0.78 us
  local copies, waits for them, and re-layouts: 12.5 us -> 4.1 us
  starting transfers between devices: 3.54 us -> 0 us
    all_gather x2 -> x0, waiting for transfers between devices: 145 us -> none  [the longest x1 77.6 us: body(): lax.all_gather(basis_in, 'seq', axis=0, tiled=True)]
    pallas_call x0 -> x1, Pallas kernels: none -> 105 us  [fused(): pl.pallas_call(kernel, out_shape=jax.ShapeDtypeStruct((128, 2048), BF16),...]
    all_to_all x2 -> x0, blocking collectives: 35.3 us -> none  [the longest x1 18.3 us: body(): lax.all_to_all(left, 'seq', split_axis=0, concat_axis=2, tiled=True)]
    dot_general x5 -> x0, matrix products: 23.5 us -> none  [the longest x1 7.1 us: body(): lax.dot_general(left_rows.reshape(cols * queries, width), full_out, (((1,...]
    all_gather x1 -> x0, blocking collectives: 20.3 us -> none  [body(): out_all = lax.all_gather(rot_out, 'seq', axis=0, tiled=True)]
    unnamed x1 -> x0, other arithmetic: 11.5 us -> none
    convert_element_type x1 -> x0, local copies, waits for them, and re-layouts: 8.14 us -> none  [body(): (raw / (QLEN * (eigvals[:, None, :] + DAMPING))).astype(jnp.bfloat16)]
    all_to_all x1 -> x0, starting transfers between devices: 3.5 us -> none  [body(): lax.all_to_all(rot_in, 'seq', split_axis=1, concat_axis=0, tiled=True)]
  transfers between devices with their start and end apart: 3 -> 0, of which waited for: 2 -> 0; matrix products, arithmetic and copies ran while one was open for 4% -> 0% of each run, Pallas kernels for 0% -> 0%
where the time goes in v1:
time: 110 us
  Pallas kernels  105 us (95%)
  local copies, waits for them, and re-layouts  4.1 us (4%)
    pallas_call x1, Pallas kernels, fused(): pl.pallas_call(kernel, out_shape=jax.ShapeDtypeStruct((128, 2048), BF16),...  105 us
    unnamed x7, local copies, waits for them, and re-layouts  4.1 us

profile of v1, /device:TPU:0, one launch (start us, length us, event | category | flops | bytes accessed | tf_op | source)
XLA Modules:
  0.0 110.1 jit_solution(17429524217397193937)
XLA Ops:
  0.0 0.8 pad_maximum_fusion.ag
  0.8 0.0 copy-start
  0.8 1.2 %copy-done = f32[128,2048]{1,0:T(8,128)S(1)} copy-done((f32[128,2048]{1,0:T(8,128)S(1)}, f32[128,2048]{1,0:T(8,128)}, u32[]{:S(2)}) %copy-start) | copy-done | bytes 1048600
  2.0 0.0 copy-start.1
  2.0 1.0 copy-done.1
  3.0 0.0 copy-start.2
  3.0 1.0 copy-done.2
  4.1 105.2 %shard_map.55 = bf16[128,2048]{1,0:T(8,128)(2,1)S(1)} custom-call(bf16[16,2048]{1,0:T(8,128)(2,1)S(1)} %pad_maximum_fusion.ag, bf16[128,2048]{1,0:T(8,128)(2,1)S(1)} %copy-done.1, bf16[128,2048]{1,0:T(8,128)(2,1)S(1)} %copy-done.2, f32[128,2048]{1,0:T(8,128)S(1)} %copy-done), custom_call_target="tpu_custom_call" | custom-call | flops 5000000000 | bytes 3000000 | tf_op jit(solution)/shard_map/pallas_call | solution.py:242
  109.3 0.8 copy.7
Async XLA Ops:
  0.8 1.2 %copy-start = (f32[128,2048]{1,0:T(8,128)S(1)}, f32[128,2048]{1,0:T(8,128)}, u32[]{:S(2)}) copy-start(f32[128,2048]{1,0:T(8,128)} %eig.1) | copy-start | bytes 3145732
  2.0 1.0 copy-start.1
  3.0 1.0 copy-start.2

commit v2 on v1

--- a/solution.py
+++ b/solution.py
@@ -17,8 +17,8 @@
     return 1 - v if d else v
 
 
-def kernel(ag, bin_, bout, eig, out,
-           ag_all, ebf, epan, bpan, binpan, part, rq, zpart, rz, rotq, rin, rout,
+def kernel(ag, bin_h, bout_h, eig_h, out,
+           bin_, bout, eig, ld, ag_all, ebf, epan, bpan, binpan, part, rq, zpart, rz, rotq, rin, rout,
            sbuf, left, leftx, psend, precv, ptmp,
            ag_s, ag_r, sl_s, sl_r, q_s, q_r, z_s, z_r, g_s, g_r,
            up_s, dn_s, blk_r, bi_s, bi_r, qy_s, qy_r, ro_s, ro_r, bo_s, bo_r, le_s, le_r, p_s, p_r):
@@ -42,6 +42,11 @@
 
     QP = ((0, 1), (1, 0), (1, 1))
 
+    loads = [pltpu.make_async_copy(a, b, ld.at[i])
+             for i, (a, b) in enumerate(((eig_h, eig), (bout_h, bout), (bin_h, bin_)))]
+    for cp in loads:
+        cp.start()
+
     barrier = pltpu.get_barrier_semaphore()
     for d in range(1, 16):
         pl.semaphore_signal(barrier, inc=1, device_id=(y, (s + d) % 16), device_id_type=MESH)
@@ -57,13 +62,15 @@
         cp.start()
         pend.append(cp)
     ag_all[s] = ag[:, pl.ds(pl.multiple_of(s * 128, 128), 128)]
+    for cp in loads:
+        cp.wait()
     ebf[...] = (1.0 / (QLEN * (eig[...] + DAMPING))).astype(BF16)
 
     rows = pl.ds(pl.multiple_of(q * 128, 128), 128)
-    for i, (dx, dc) in enumerate(QP):
-        xx, cc = flip(x, dx), flip(c, dc)
-        cols = pl.ds(pl.multiple_of((xx * 4 + cc * 2 + y) * 256, 256), 256)
-        for k, (src, dst) in enumerate(((ebf, epan), (bout, bpan.at[0]))):
+    for k, (src, dst) in enumerate(((ebf, epan), (bout, bpan.at[0]))):
+        for i, (dx, dc) in enumerate(QP):
+            xx, cc = flip(x, dx), flip(c, dc)
+            cols = pl.ds(pl.multiple_of((xx * 4 + cc * 2 + y) * 256, 256), 256)
             cp = rc(src.at[:, cols], dst.at[z, rows], sl_s.at[i, k], sl_r.at[i, k], dev(z, xx, cc, y))
             cp.start()
             pend.append(cp)
@@ -91,21 +98,43 @@
         arrived(epan.at[z, src], sl_r.at[i, 0])
         arrived(bpan.at[0, z, src], sl_r.at[i, 1])
 
-    def hop(j):
+    pans = (epan, bpan.at[0])
+
+    def share(b):
+        for i, to in ((1, dev(z, x, 1 - c, y)), (2, dev(z, x, c, 1 - y))):
+            rc(bpan.at[0, b], bpan.at[i, b], bo_s.at[i, b], bo_r.at[i, b], to).start()
+
+    def hop(j, k):
+        ref = pans[k]
         for up, sems in ((True, up_s), (False, dn_s)):
             b = z - j if up else z + j
             ok = (b >= 0) if up else (b <= 3)
             nxt = z + 1 if up else z - 1
             can = (z < 3) if up else (z > 0)
-            for k, ref in enumerate((epan, bpan.at[0])):
-                if j > 0:
-                    @pl.when(ok)
-                    def _():
-                        arrived(ref.at[b], blk_r.at[b, k])
-                if j < 3:
-                    @pl.when(ok & can)
-                    def _():
-                        rc(ref.at[b], ref.at[b], sems.at[j, k], blk_r.at[b, k], dev(nxt, x, c, y)).start()
+            if j > 0:
+                @pl.when(ok)
+                def _():
+                    arrived(ref.at[b], blk_r.at[b, k])
+            if j < 3:
+                @pl.when(ok & can)
+                def _():
+                    rc(ref.at[b], ref.at[b], sems.at[j, k], blk_r.at[b, k], dev(nxt, x, c, y)).start()
+            if k == 1 and j > 0:
+                @pl.when(ok)
+                def _():
+                    share(b)
+        if k == 1 and j == 0:
+            share(z)
+
+    def onward(j):
+        for up in ((True, False) if j else (True,)):
+            b = z - j if up else z + j
+            ok = (b >= 0) if up else (b <= 3)
+
+            @pl.when(ok)
+            def _():
+                arrived(bpan.at[2, b], bo_r.at[2, b])
+                rc(bpan.at[2, b], bpan.at[3, b], bo_s.at[3, b], bo_r.at[3, b], dev(z, x, 1 - c, y)).start()
 
     def hop_sent():
         for j in range(3):
@@ -116,10 +145,14 @@
 
                 @pl.when(ok & can)
                 def _():
-                    for k, ref in enumerate((epan, bpan.at[0])):
-                        sent(ref.at[b], sems.at[j, k])
-
-    hop(0)
+                    for k in range(2):
+                        sent(pans[k].at[b], sems.at[j, k])
+        for i in range(1, 4):
+            for b in range(4):
+                sent(bpan.at[i, b], bo_s.at[i, b])
+
+    hop(0, 0)
+    hop(0, 1)
 
     tot = part[q].astype(F32)
     for i in range(3):
@@ -150,7 +183,7 @@
         cp = rc(rotq.at[z], rotq.at[z], g_s.at[d], g_r.at[4 - d], dev(zz, x, c, y))
         cp.start()
         pend.append(cp)
-    hop(1)
+    hop(1, 0)
     for d in range(1, 4):
         arrived(rotq.at[(z + d) % 4], g_r.at[d])
 
@@ -173,12 +206,10 @@
     cp.start()
     pend.append(cp)
 
-    hop(2)
-    hop(3)
-    for i, to in ((1, dev(z, x, 1 - c, y)), (2, dev(z, x, c, 1 - y))):
-        cp = rc(bpan.at[0], bpan.at[i], bo_s.at[i], bo_r.at[i], to)
-        cp.start()
-        pend.append(cp)
+    hop(2, 0)
+    hop(1, 1)
+    onward(0)
+    hop(3, 0)
 
     for i in range(1, 8):
         dy, dx, dc = i // 4, (i // 2) % 2, i % 2
@@ -193,42 +224,51 @@
                 e = epan[m, t * 128:(t + 1) * 128].astype(F32)
                 sbuf[m * 512 + t * 128:m * 512 + (t + 1) * 128, g * 256:(g + 1) * 256] = (raw * e).astype(BF16)
 
+    hop(2, 1)
+    onward(1)
     arrived(binpan.at[(1 - c) * 2 + x], bi_r.at[0])
     arrived(binpan.at[(1 - c) * 2 + 1 - x], bi_r.at[2])
-    for i in range(4):
-        l = jnp.dot(binpan[i], sbuf[...], preferred_element_type=F32).astype(BF16)
-        left[0, i] = l[:, :256]
-        left[1, i] = l[:, 256:]
+    for h, xr in enumerate((1 - x, x)):
+        for cc in range(2):
+            l = jnp.dot(binpan[cc * 2 + xr], sbuf[...], preferred_element_type=F32).astype(BF16)
+            left[h, 0, cc] = l[:, :256]
+            left[h, 1, cc] = l[:, 256:]
+        for i in range(1, 4):
+            dy, dc = i // 2, i % 2
+            yy, cc = flip(y, dy), flip(c, dc)
+            cp = rc(left.at[h, yy, cc], leftx.at[h, i], le_s.at[h, i], le_r.at[h, i], dev(z, x, cc, yy))
+            cp.start()
+            pend.append(cp)
+        leftx[h, 0] = left[h, y, c]
+    hop(3, 1)
+
+    def product(h, n):
+        acc = jnp.zeros((128, 512), F32)
+        for i in range(4):
+            acc = acc + lax.dot_general(leftx[h, i], bpan[i, n], (((1,), (1,)), ((), ())),
+                                        preferred_element_type=F32)
+        return acc
+
+    order = [z, z + 1 - 2 * (z % 2), (z + 2) % 4, 3 - z]
     for i in range(1, 4):
-        dy, dc = i // 2, i % 2
-        yy, cc = flip(y, dy), flip(c, dc)
-        cp = rc(left.at[yy, pl.ds(cc * 2, 2)], leftx.at[i], le_s.at[i], le_r.at[i], dev(z, x, cc, yy))
-        cp.start()
-        pend.append(cp)
-    leftx[0] = left[y, pl.ds(c * 2, 2)]
-
-    arrived(bpan.at[2], bo_r.at[2])
-    cp = rc(bpan.at[2], bpan.at[3], bo_s.at[3], bo_r.at[3], dev(z, x, 1 - c, y))
-    cp.start()
-    pend.append(cp)
-    arrived(bpan.at[1], bo_r.at[1])
+        arrived(leftx.at[0, i], le_r.at[0, i])
+    for k, n in enumerate(order):
+        if k == 2:
+            onward(2)
+            onward(3)
+        arrived(bpan.at[1, n], bo_r.at[1, n])
+        arrived(bpan.at[3, n], bo_r.at[3, n])
+        psend[k] = product(0, n).astype(BF16)
+        cp = rc(psend.at[k], precv.at[k], p_s.at[k], p_r.at[k], dev(z, 1 - x, c, y))
+        cp.start()
+        pend.append(cp)
     for i in range(1, 4):
-        arrived(leftx.at[i], le_r.at[i])
-    arrived(bpan.at[3], bo_r.at[3])
-
-    for n in range(4):
-        acc = jnp.zeros((256, 512), F32)
-        for i in range(4):
-            acc = acc + lax.dot_general(leftx[i].reshape(256, 256), bpan[i, n], (((1,), (1,)), ((), ())),
-                                        preferred_element_type=F32)
-        ptmp[n] = acc.reshape(2, 128, 512)
-        psend[n] = ptmp[n, 1 - x].astype(BF16)
-        cp = rc(psend.at[n], precv.at[n], p_s.at[n], p_r.at[n], dev(z, 1 - x, c, y))
-        cp.start()
-        pend.append(cp)
-    for n in range(4):
-        arrived(precv.at[n], p_r.at[n])
-        out[:, n * 512:(n + 1) * 512] = (ptmp[n, x] + precv[n].astype(F32)).astype(BF16)
+        arrived(leftx.at[1, i], le_r.at[1, i])
+    for k, n in enumerate(order):
+        ptmp[k] = product(1, n)
+    for k, n in enumerate(order):
+        arrived(precv.at[k], p_r.at[k])
+        out[:, pl.ds(pl.multiple_of(n * 512, 512), 512)] = (ptmp[k] + precv[k].astype(F32)).astype(BF16)
 
     for cp in pend:
         cp.wait_send()
@@ -242,17 +282,18 @@
     out = pl.pallas_call(
         kernel,
         out_shape=jax.ShapeDtypeStruct((128, 2048), BF16),
-        in_specs=[pl.BlockSpec(memory_space=v)] * 4,
+        in_specs=[pl.BlockSpec(memory_space=v)] + [pl.BlockSpec(memory_space=pltpu.MemorySpace.HBM)] * 3,
         out_specs=pl.BlockSpec(memory_space=v),
         scratch_shapes=[
+            v((128, 2048), BF16), v((128, 2048), BF16), v((128, 2048), F32), dma(3),
             v((16, 16, 128), BF16), v((128, 2048), BF16), v((4, 512, 256), BF16), v((4, 4, 512, 256), BF16),
             v((4, 128, 2048), BF16), v((4, 256, 512), BF16), v((3, 256, 512), BF16), v((4, 256, 128), BF16),
             v((4, 256, 128), BF16), v((4, 256, 128), BF16), v((2, 4, 4, 128, 128), BF16), v((2, 2, 128, 128), BF16),
-            v((2048, 512), BF16), v((2, 4, 128, 256), BF16), v((4, 2, 128, 256), BF16),
-            v((4, 128, 512), BF16), v((4, 128, 512), BF16), v((4, 2, 128, 512), F32),
+            v((2048, 512), BF16), v((2, 2, 2, 128, 256), BF16), v((2, 4, 128, 256), BF16),
+            v((4, 128, 512), BF16), v((4, 128, 512), BF16), v((4, 128, 512), F32),
             dma(16), dma(16), dma(3, 2), dma(3, 2), dma(3), dma(3), dma(4), dma(4), dma(4), dma(4),
-            dma(3, 2), dma(3, 2), dma(4, 2), dma(3), dma(3), dma(8), dma(8), dma(1), dma(1), dma(4), dma(4),
-            dma(4), dma(4), dma(4), dma(4),
+            dma(3, 2), dma(3, 2), dma(4, 2), dma(3), dma(3), dma(8), dma(8), dma(1), dma(1), dma(4, 4), dma(4, 4),
+            dma(2, 4), dma(2, 4), dma(4), dma(4),
         ],
         compiler_params=pltpu.CompilerParams(
             collective_id=0, has_side_effects=True, vmem_limit_bytes=48 * 1024 * 1024),

time: 110 us -> 92.2 us (0.84)
  the two profiles are of different devices: /device:TPU:0 before, /device:TPU:9 now
where the time goes in v2:
time: 92.2 us; the launch traced here: 91.8 us
  Pallas kernels  87 us (94%)
  local copies, waits for them, and re-layouts  4.1 us (4%)
    pallas_call x1, Pallas kernels, fused(): pl.pallas_call(kernel, out_shape=jax.ShapeDtypeStruct((128, 2048), BF16),...  87 us
    unnamed x7, local copies, waits for them, and re-layouts  4.1 us

profile of v2, /device:TPU:9, one launch (start us, length us, event | category | flops | bytes accessed | tf_op | source)
XLA Modules:
  0.0 91.8 jit_solution(11152680657400172158)
XLA Ops:
  0.0 0.8 pad_maximum_fusion.ag
  0.8 0.0 copy-start
  0.8 1.2 %copy-done = f32[128,2048]{1,0:T(8,128)S(1)} copy-done((f32[128,2048]{1,0:T(8,128)S(1)}, f32[128,2048]{1,0:T(8,128)}, u32[]{:S(2)}) %copy-start) | copy-done | bytes 1048600
  2.0 0.0 copy-start.1
  2.0 1.0 %copy-done.1 = bf16[128,2048]{1,0:T(8,128)(2,1)S(1)} copy-done((bf16[128,2048]{1,0:T(8,128)(2,1)S(1)}, bf16[128,2048]{1,0:T(8,128)(2,1)}, u32[]{:S(2)}) %copy-start.1) | copy-done | bytes 524312
  3.0 0.0 copy-start.2
  3.0 1.0 %copy-done.2 = bf16[128,2048]{1,0:T(8,128)(2,1)S(1)} copy-done((bf16[128,2048]{1,0:T(8,128)(2,1)S(1)}, bf16[128,2048]{1,0:T(8,128)(2,1)}, u32[]{:S(2)}) %copy-start.2) | copy-done | bytes 524312
  4.1 87.0 %shard_map.55 = bf16[128,2048]{1,0:T(8,128)(2,1)S(1)} custom-call(bf16[16,2048]{1,0:T(8,128)(2,1)S(1)} %pad_maximum_fusion.ag, bf16[128,2048]{1,0:T(8,128)(2,1)S(1)} %copy-done.1, bf16[128,2048]{1,0:T(8,128)(2,1)S(1)} %copy-done.2, f32[128,2048]{1,0:T(8,128)S(1)} %copy-done), custom_call_target="tpu_custom_call" | custom-call | flops 5000000000 | bytes 3000000 | tf_op jit(solution)/shard_map/pallas_call | solution.py:282
  91.1 0.8 copy.7
Async XLA Ops:
  0.8 1.2 %copy-start = (f32[128,2048]{1,0:T(8,128)S(1)}, f32[128,2048]{1,0:T(8,128)}, u32[]{:S(2)}) copy-start(f32[128,2048]{1,0:T(8,128)} %eig_h.1) | copy-start | bytes 3145732
  2.0 1.0 %copy-start.1 = (bf16[128,2048]{1,0:T(8,128)(2,1)S(1)}, bf16[128,2048]{1,0:T(8,128)(2,1)}, u32[]{:S(2)}) copy-start(bf16[128,2048]{1,0:T(8,128)(2,1)} %bin_h.1) | copy-start | bytes 1572868
  3.0 1.0 %copy-start.2 = (bf16[128,2048]{1,0:T(8,128)(2,1)S(1)}, bf16[128,2048]{1,0:T(8,128)(2,1)}, u32[]{:S(2)}) copy-start(bf16[128,2048]{1,0:T(8,128)(2,1)} %bout_h.1) | copy-start | bytes 1572868

commit v3 on v2

--- a/solution.py
+++ b/solution.py
@@ -18,7 +18,7 @@
 
 
 def kernel(ag, bin_h, bout_h, eig_h, out,
-           bin_, bout, eig, ld, ag_all, ebf, epan, bpan, binpan, part, rq, zpart, rz, rotq, rin, rout,
+           bin_, bout, eig, ld, ag_all, ebf, epan, bpan, binpan, part, rq, zown, zpart, rz, rotq, rin, rout,
            sbuf, left, leftx, psend, precv, ptmp,
            ag_s, ag_r, sl_s, sl_r, q_s, q_r, z_s, z_r, g_s, g_r,
            up_s, dn_s, blk_r, bi_s, bi_r, qy_s, qy_r, ro_s, ro_r, bo_s, bo_r, le_s, le_r, p_s, p_r):
@@ -67,13 +67,17 @@
     ebf[...] = (1.0 / (QLEN * (eig[...] + DAMPING))).astype(BF16)
 
     rows = pl.ds(pl.multiple_of(q * 128, 128), 128)
-    for k, (src, dst) in enumerate(((ebf, epan), (bout, bpan.at[0]))):
+
+    def slices(k):
+        src, dst = ((ebf, epan), (bout, bpan.at[0]))[k]
         for i, (dx, dc) in enumerate(QP):
             xx, cc = flip(x, dx), flip(c, dc)
             cols = pl.ds(pl.multiple_of((xx * 4 + cc * 2 + y) * 256, 256), 256)
             cp = rc(src.at[:, cols], dst.at[z, rows], sl_s.at[i, k], sl_r.at[i, k], dev(z, xx, cc, y))
             cp.start()
             pend.append(cp)
+
+    slices(0)
     own = pl.ds(pl.multiple_of((q * 2 + y) * 256, 256), 256)
     epan[z, rows] = ebf[:, own]
     bpan[0, z, rows] = bout[:, own]
@@ -81,22 +85,23 @@
     for d in range(1, 16):
         arrived(ag_all.at[(s + d) % 16], ag_r.at[d])
     tok = ag_all[...].reshape(256, 128)
-    for n in range(4):
-        cs = slice(n * 512, n * 512 + 512)
-        a = jnp.dot(tok, bin_[:, cs], preferred_element_type=F32).reshape(16, 16, 512)
-        part[n, :128] = a[:, :8].reshape(128, 512).astype(BF16)
-        b = jnp.dot(tok, bout[:, cs], preferred_element_type=F32).reshape(16, 16, 512)
-        part[n, 128:] = b[:, 8:].reshape(128, 512).astype(BF16)
-    for i, (dx, dc) in enumerate(QP):
-        xx, cc = flip(x, dx), flip(c, dc)
-        cp = rc(part.at[xx * 2 + cc], rq.at[i], q_s.at[i], q_r.at[i], dev(z, xx, cc, y))
-        cp.start()
-        pend.append(cp)
-
-    for i, (dx, dc) in enumerate(QP):
-        src = pl.ds(pl.multiple_of((flip(x, dx) * 2 + flip(c, dc)) * 128, 128), 128)
-        arrived(epan.at[z, src], sl_r.at[i, 0])
-        arrived(bpan.at[0, z, src], sl_r.at[i, 1])
+    for h, basis in enumerate((bin_, bout)):
+        for n in range(4):
+            a = jnp.dot(tok, basis[:, n * 512:(n + 1) * 512], preferred_element_type=F32).reshape(16, 16, 512)
+            part[n, h * 128:(h + 1) * 128] = a[:, h * 8:(h + 1) * 8].reshape(128, 512).astype(BF16)
+        half = pl.ds(h * 128, 128)
+        for i, (dx, dc) in enumerate(QP):
+            xx, cc = flip(x, dx), flip(c, dc)
+            cp = rc(part.at[xx * 2 + cc, half], rq.at[i, half], q_s.at[i, h], q_r.at[i, h], dev(z, xx, cc, y))
+            cp.start()
+            pend.append(cp)
+        if h == 0:
+            slices(1)
+
+    def slices_in(k):
+        for i, (dx, dc) in enumerate(QP):
+            src = pl.ds(pl.multiple_of((flip(x, dx) * 2 + flip(c, dc)) * 128, 128), 128)
+            arrived(pans[k].at[z, src], sl_r.at[i, k])
 
     pans = (epan, bpan.at[0])
 
@@ -151,20 +156,61 @@
             for b in range(4):
                 sent(bpan.at[i, b], bo_s.at[i, b])
 
+    def plane_sum(h):
+        half = slice(h * 128, (h + 1) * 128)
+        tot = part[q, half].astype(F32)
+        for i in range(3):
+            arrived(rq.at[i, pl.ds(h * 128, 128)], q_r.at[i, h])
+            tot = tot + rq[i, half].astype(F32)
+        for i in range(4):
+            zown[h, i] = tot[:, i * 128:(i + 1) * 128]
+            zpart[h, i] = tot[:, i * 128:(i + 1) * 128].astype(BF16)
+        for d in range(1, 4):
+            zz = (z + d) % 4
+            cp = rc(zpart.at[h, zz], rz.at[h, 4 - d], z_s.at[h, d], z_r.at[h, 4 - d], dev(zz, x, c, y))
+            cp.start()
+            pend.append(cp)
+
+    def line_sum(h):
+        tot = zown[h, z]
+        for d in range(1, 4):
+            arrived(rz.at[h, d], z_r.at[h, d])
+            tot = tot + rz[h, d].astype(F32)
+        rotq[h, z] = tot.astype(BF16)
+        for d in range(1, 4):
+            zz = (z + d) % 4
+            cp = rc(rotq.at[h, z], rotq.at[h, z], g_s.at[h, d], g_r.at[h, 4 - d], dev(zz, x, c, y))
+            cp.start()
+            pend.append(cp)
+
+    FAR = ((1, 0, 1), (2, 1, 0), (3, 1, 1))
+
+    def spread(k):
+        b = (z + k) % 4
+        rin[y, q, b] = rotq[0, b]
+        for i, dy, dx in ((0, 0, 0),) + FAR:
+            cp = rc(rotq.at[0, b], rin.at[y, q, b], qy_s.at[i, k], qy_r.at[i, k],
+                    dev(z, flip(x, dx), c if i else 1 - c, flip(y, dy)))
+            cp.start()
+            pend.append(cp)
+
+    def spread_on(k):
+        b = (z + k) % 4
+        for i, dy, dx in FAR:
+            ref = rin.at[flip(y, dy), flip(x, dx) * 2 + c, b]
+            arrived(ref, qy_r.at[i, k])
+            cp = rc(ref, ref, qy_s.at[3 + i, k], qy_r.at[3 + i, k], dev(z, x, 1 - c, y))
+            cp.start()
+            pend.append(cp)
+
+    plane_sum(0)
+    slices_in(0)
     hop(0, 0)
+    plane_sum(1)
+    line_sum(0)
+    spread(0)
+    slices_in(1)
     hop(0, 1)
-
-    tot = part[q].astype(F32)
-    for i in range(3):
-        arrived(rq.at[i], q_r.at[i])
-        tot = tot + rq[i].astype(F32)
-    for i in range(4):
-        zpart[i] = tot[:, i * 128:(i + 1) * 128].astype(BF16)
-    for d in range(1, 4):
-        zz = (z + d) % 4
-        cp = rc(zpart.at[zz], rz.at[4 - d], z_s.at[d], z_r.at[4 - d], dev(zz, x, c, y))
-        cp.start()
-        pend.append(cp)
 
     slot = c * 2 + x
     binpan[slot] = bin_[...]
@@ -173,32 +219,20 @@
         cp.start()
         pend.append(cp)
 
-    tot = zpart[z].astype(F32)
-    for d in range(1, 4):
-        arrived(rz.at[d], z_r.at[d])
-        tot = tot + rz[d].astype(F32)
-    rotq[z] = tot.astype(BF16)
-    for d in range(1, 4):
-        zz = (z + d) % 4
-        cp = rc(rotq.at[z], rotq.at[z], g_s.at[d], g_r.at[4 - d], dev(zz, x, c, y))
-        cp.start()
-        pend.append(cp)
+    line_sum(1)
+    for k in range(1, 4):
+        arrived(rotq.at[0, (z + k) % 4], g_r.at[0, k])
+        spread(k)
+    spread_on(0)
     hop(1, 0)
-    for d in range(1, 4):
-        arrived(rotq.at[(z + d) % 4], g_r.at[d])
-
-    rin[y, q] = rotq[:, :128]
-    rout[y] = rotq[pl.ds(2 * y, 2), 128:]
-    for i in range(1, 8):
-        dy, dx, dc = i // 4, (i // 2) % 2, i % 2
-        cp = rc(rotq.at[:, pl.ds(0, 128)], rin.at[y, q], qy_s.at[i], qy_r.at[i],
-                dev(z, flip(x, dx), flip(c, dc), flip(y, dy)))
-        cp.start()
-        pend.append(cp)
-    cp = rc(rotq.at[pl.ds(2 * (1 - y), 2), pl.ds(128, 128)], rout.at[y], ro_s.at[0], ro_r.at[0],
-            dev(z, x, c, 1 - y))
+    for k in range(1, 4):
+        arrived(rotq.at[1, (z + k) % 4], g_r.at[1, k])
+    rout[y] = rotq[1, pl.ds(2 * y, 2)]
+    cp = rc(rotq.at[1, pl.ds(2 * (1 - y), 2)], rout.at[y], ro_s.at[0], ro_r.at[0], dev(z, x, c, 1 - y))
     cp.start()
     pend.append(cp)
+    for k in range(1, 4):
+        spread_on(k)
 
     far = c * 2 + 1 - x
     arrived(binpan.at[far], bi_r.at[1])
@@ -211,9 +245,11 @@
     onward(0)
     hop(3, 0)
 
-    for i in range(1, 8):
-        dy, dx, dc = i // 4, (i // 2) % 2, i % 2
-        arrived(rin.at[flip(y, dy), flip(x, dx) * 2 + flip(c, dc)], qy_r.at[i])
+    for k in range(4):
+        b = (z + k) % 4
+        arrived(rin.at[y, x * 2 + 1 - c, b], qy_r.at[0, k])
+        for i, dy, dx in FAR:
+            arrived(rin.at[flip(y, dy), flip(x, dx) * 2 + 1 - c, b], qy_r.at[3 + i, k])
     arrived(rout.at[1 - y], ro_r.at[0])
 
     for g in range(2):
@@ -287,12 +323,12 @@
         scratch_shapes=[
             v((128, 2048), BF16), v((128, 2048), BF16), v((128, 2048), F32), dma(3),
             v((16, 16, 128), BF16), v((128, 2048), BF16), v((4, 512, 256), BF16), v((4, 4, 512, 256), BF16),
-            v((4, 128, 2048), BF16), v((4, 256, 512), BF16), v((3, 256, 512), BF16), v((4, 256, 128), BF16),
-            v((4, 256, 128), BF16), v((4, 256, 128), BF16), v((2, 4, 4, 128, 128), BF16), v((2, 2, 128, 128), BF16),
+            v((4, 128, 2048), BF16), v((4, 256, 512), BF16), v((3, 256, 512), BF16), v((2, 4, 128, 128), F32), v((2, 4, 128, 128), BF16),
+            v((2, 4, 128, 128), BF16), v((2, 4, 128, 128), BF16), v((2, 4, 4, 128, 128), BF16), v((2, 2, 128, 128), BF16),
             v((2048, 512), BF16), v((2, 2, 2, 128, 256), BF16), v((2, 4, 128, 256), BF16),
             v((4, 128, 512), BF16), v((4, 128, 512), BF16), v((4, 128, 512), F32),
-            dma(16), dma(16), dma(3, 2), dma(3, 2), dma(3), dma(3), dma(4), dma(4), dma(4), dma(4),
-            dma(3, 2), dma(3, 2), dma(4, 2), dma(3), dma(3), dma(8), dma(8), dma(1), dma(1), dma(4, 4), dma(4, 4),
+            dma(16), dma(16), dma(3, 2), dma(3, 2), dma(3, 2), dma(3, 2), dma(2, 4), dma(2, 4), dma(2, 4), dma(2, 4),
+            dma(3, 2), dma(3, 2), dma(4, 2), dma(3), dma(3), dma(7, 4), dma(7, 4), dma(1), dma(1), dma(4, 4), dma(4, 4),
             dma(2, 4), dma(2, 4), dma(4), dma(4),
         ],
         compiler_params=pltpu.CompilerParams(

time: 92.2 us -> 94.2 us (1.022)
  the two profiles are of different devices: /device:TPU:9 before, /device:TPU:0 now
where the time goes in v3:
time: 94.2 us; the launch traced here: 93.9 us
  Pallas kernels  89 us (94%)
  local copies, waits for them, and re-layouts  4.1 us (4%)
    pallas_call x1, Pallas kernels, fused(): pl.pallas_call(kernel, out_shape=jax.ShapeDtypeStruct((128, 2048), BF16),...  89 us
    unnamed x7, local copies, waits for them, and re-layouts  4.1 us

profile of v3, /device:TPU:0, one launch (start us, length us, event | category | flops | bytes accessed | tf_op | source)
XLA Modules:
  0.0 93.9 jit_solution(1388894339328385303)
XLA Ops:
  0.0 0.8 pad_maximum_fusion.ag
  0.8 0.0 copy-start
  0.8 1.2 %copy-done = f32[128,2048]{1,0:T(8,128)S(1)} copy-done((f32[128,2048]{1,0:T(8,128)S(1)}, f32[128,2048]{1,0:T(8,128)}, u32[]{:S(2)}) %copy-start) | copy-done | bytes 1048600
  2.0 0.0 copy-start.1
  2.0 1.0 %copy-done.1 = bf16[128,2048]{1,0:T(8,128)(2,1)S(1)} copy-done((bf16[128,2048]{1,0:T(8,128)(2,1)S(1)}, bf16[128,2048]{1,0:T(8,128)(2,1)}, u32[]{:S(2)}) %copy-start.1) | copy-done | bytes 524312
  3.0 0.0 copy-start.2
  3.0 1.0 %copy-done.2 = bf16[128,2048]{1,0:T(8,128)(2,1)S(1)} copy-done((bf16[128,2048]{1,0:T(8,128)(2,1)S(1)}, bf16[128,2048]{1,0:T(8,128)(2,1)}, u32[]{:S(2)}) %copy-start.2) | copy-done | bytes 524312
  4.1 89.0 %shard_map.55 = bf16[128,2048]{1,0:T(8,128)(2,1)S(1)} custom-call(bf16[16,2048]{1,0:T(8,128)(2,1)S(1)} %pad_maximum_fusion.ag, bf16[128,2048]{1,0:T(8,128)(2,1)S(1)} %copy-done.1, bf16[128,2048]{1,0:T(8,128)(2,1)S(1)} %copy-done.2, f32[128,2048]{1,0:T(8,128)S(1)} %copy-done), custom_call_target="tpu_custom_call" | custom-call | flops 5000000000 | bytes 3000000 | tf_op jit(solution)/shard_map/pallas_call | solution.py:318
  93.1 0.8 copy.7
Async XLA Ops:
  0.8 1.2 %copy-start = (f32[128,2048]{1,0:T(8,128)S(1)}, f32[128,2048]{1,0:T(8,128)}, u32[]{:S(2)}) copy-start(f32[128,2048]{1,0:T(8,128)} %eig_h.1) | copy-start | bytes 3145732
  2.0 1.0 %copy-start.1 = (bf16[128,2048]{1,0:T(8,128)(2,1)S(1)}, bf16[128,2048]{1,0:T(8,128)(2,1)}, u32[]{:S(2)}) copy-start(bf16[128,2048]{1,0:T(8,128)(2,1)} %bin_h.1) | copy-start | bytes 1572868
  3.0 1.0 %copy-start.2 = (bf16[128,2048]{1,0:T(8,128)(2,1)S(1)}, bf16[128,2048]{1,0:T(8,128)(2,1)}, u32[]{:S(2)}) copy-start(bf16[128,2048]{1,0:T(8,128)(2,1)} %bout_h.1) | copy-start | bytes 1572868

commit v4 on v3

--- a/solution.py
+++ b/solution.py
@@ -203,14 +203,15 @@
             cp.start()
             pend.append(cp)
 
-    plane_sum(0)
     slices_in(0)
     hop(0, 0)
+    plane_sum(0)
+    slices_in(1)
+    hop(0, 1)
     plane_sum(1)
     line_sum(0)
     spread(0)
-    slices_in(1)
-    hop(0, 1)
+    hop(1, 0)
 
     slot = c * 2 + x
     binpan[slot] = bin_[...]
@@ -223,8 +224,9 @@
     for k in range(1, 4):
         arrived(rotq.at[0, (z + k) % 4], g_r.at[0, k])
         spread(k)
+    hop(2, 0)
+    hop(1, 1)
     spread_on(0)
-    hop(1, 0)
     for k in range(1, 4):
         arrived(rotq.at[1, (z + k) % 4], g_r.at[1, k])
     rout[y] = rotq[1, pl.ds(2 * y, 2)]
@@ -240,8 +242,6 @@
     cp.start()
     pend.append(cp)
 
-    hop(2, 0)
-    hop(1, 1)
     onward(0)
     hop(3, 0)
 

time: 94.2 us -> 87.2 us (0.926)
  Pallas kernels: 89 us -> 82 us
    pallas_call x1, Pallas kernels: 89 us -> 82 us  [fused(): pl.pallas_call(kernel, out_shape=jax.ShapeDtypeStruct((128, 2048), BF16),...]
where the time goes in v4:
time: 87.2 us; the launch traced here: 86.9 us
  Pallas kernels  82 us (94%)
  local copies, waits for them, and re-layouts  4.1 us (5%)
    pallas_call x1, Pallas kernels, fused(): pl.pallas_call(kernel, out_shape=jax.ShapeDtypeStruct((128, 2048), BF16),...  82 us
    unnamed x7, local copies, waits for them, and re-layouts  4.1 us

profile of v4, /device:TPU:0, one launch (start us, length us, event | category | flops | bytes accessed | tf_op | source)
XLA Modules:
  0.0 86.9 jit_solution(4343809727431371373)
XLA Ops:
  0.0 0.8 pad_maximum_fusion.ag
  0.8 0.0 copy-start
  0.8 1.2 %copy-done = f32[128,2048]{1,0:T(8,128)S(1)} copy-done((f32[128,2048]{1,0:T(8,128)S(1)}, f32[128,2048]{1,0:T(8,128)}, u32[]{:S(2)}) %copy-start) | copy-done | bytes 1048600
  2.0 0.0 copy-start.1
  2.0 1.0 %copy-done.1 = bf16[128,2048]{1,0:T(8,128)(2,1)S(1)} copy-done((bf16[128,2048]{1,0:T(8,128)(2,1)S(1)}, bf16[128,2048]{1,0:T(8,128)(2,1)}, u32[]{:S(2)}) %copy-start.1) | copy-done | bytes 524312
  3.0 0.0 copy-start.2
  3.0 1.0 %copy-done.2 = bf16[128,2048]{1,0:T(8,128)(2,1)S(1)} copy-done((bf16[128,2048]{1,0:T(8,128)(2,1)S(1)}, bf16[128,2048]{1,0:T(8,128)(2,1)}, u32[]{:S(2)}) %copy-start.2) | copy-done | bytes 524312
  4.1 82.0 %shard_map.55 = bf16[128,2048]{1,0:T(8,128)(2,1)S(1)} custom-call(bf16[16,2048]{1,0:T(8,128)(2,1)S(1)} %pad_maximum_fusion.ag, bf16[128,2048]{1,0:T(8,128)(2,1)S(1)} %copy-done.1, bf16[128,2048]{1,0:T(8,128)(2,1)S(1)} %copy-done.2, f32[128,2048]{1,0:T(8,128)S(1)} %copy-done), custom_call_target="tpu_custom_call" | custom-call | flops 5000000000 | bytes 3000000 | tf_op jit(solution)/shard_map/pallas_call | solution.py:318
  86.1 0.8 copy.7
Async XLA Ops:
  0.8 1.2 %copy-start = (f32[128,2048]{1,0:T(8,128)S(1)}, f32[128,2048]{1,0:T(8,128)}, u32[]{:S(2)}) copy-start(f32[128,2048]{1,0:T(8,128)} %eig_h.1) | copy-start | bytes 3145732
  2.0 1.0 %copy-start.1 = (bf16[128,2048]{1,0:T(8,128)(2,1)S(1)}, bf16[128,2048]{1,0:T(8,128)(2,1)}, u32[]{:S(2)}) copy-start(bf16[128,2048]{1,0:T(8,128)(2,1)} %bin_h.1) | copy-start | bytes 1572868
  3.0 1.0 %copy-start.2 = (bf16[128,2048]{1,0:T(8,128)(2,1)S(1)}, bf16[128,2048]{1,0:T(8,128)(2,1)}, u32[]{:S(2)}) copy-start(bf16[128,2048]{1,0:T(8,128)(2,1)} %bout_h.1) | copy-start | bytes 1572868
